TPU v7x, 32 devices: a whole 2x2x4 slice. The times are simulated.
32 devices in a mesh: ctx: 4 (over y, x), head: 8 (over z, core).
Axes of the slice: x: 2, y: 2, z: 4, core: 2. Of those that a mesh axis runs over, the one named last changes fastest.
Arguments:
- queries: bfloat16 [4096, 4096], P('ctx', 'head'), may hold values from -6 to 6
- key_heads: bfloat16 [4096, 4096], P('ctx', 'head'), may hold values from -8 to 8
- value_heads: bfloat16 [4096, 4096], P('ctx', 'head'), may hold values from -120 to 120
- out_gain: bfloat16 [4096], P('head'), may hold values from 0.099609375 to 1.8984375
- out_weight: bfloat16 [4096, 2048], P('head'), may hold values from -0.09375 to 0.09375
- residual: bfloat16 [4096, 2048], P(('ctx', 'head')), may hold values from -36 to 36
- norm_gain: bfloat16 [2048], replicated, may hold values from 0.099609375 to 1.8984375
- routes: int32 [4096, 8], P(('ctx', 'head')), may hold values from 0 to 127, all different within a row; in each aligned block of 128 rows (0 to 127, 128 to 255, ...) at most 10 rows name the same one
- route_weights: float32 [4096, 8], P(('ctx', 'head')), may hold values from 0.02 to 0.4
- cotangent: bfloat16 [4096, 2048], P(('ctx', 'head')), may hold values from -6 to 6
- w_gate: bfloat16 [128, 2048, 768], P(('ctx', 'head')), may hold values from -0.125 to 0.125
- w_up: bfloat16 [128, 2048, 768], P(('ctx', 'head')), may hold values from -0.125 to 0.125
- w_down: bfloat16 [128, 768, 2048], P(('ctx', 'head')), may hold values from -0.21875 to 0.21875
Outputs:
- hidden_out: bfloat16 [4096, 2048], P(('ctx', 'head'))
- grad_gate: bfloat16 [128, 2048, 768], P(('ctx', 'head'))
- grad_up: bfloat16 [128, 2048, 768], P(('ctx', 'head'))
- grad_down: bfloat16 [128, 768, 2048], P(('ctx', 'head'))
Inputs may be any that keep to these rules, and one draw needn't show every extreme that they name: `routes`: each row names 8 different experts. Within each aligned block of 128 rows no expert is named by more than 10 rows; in some blocks an expert is named by exactly 10 rows.
All inputs are finite; a program needn't handle non-finite values.
Results may differ from a plain program's by a relative error of at most 0.025.
Values may be sent and summed in bfloat16 or wider, within the bound.
A program may use at most 192 MiB of HBM per device.

v0:
```python
import jax
import jax.numpy as jnp
from jax import lax
from jax.sharding import PartitionSpec as P

HEADS = 32
HD = 128
EXPERTS = 128
TOPK = 8


epsilon = 1e-06
highest = lax.Precision.HIGHEST


def carried_in(value, axis, join, neutral):
    place = lax.axis_index(axis)
    gathered = jax.tree.map(
        lambda a, kind: lax.all_gather(a.astype(kind), axis), value, (jnp.bfloat16, jnp.bfloat16)
    )
    state = jax.tree.map(lambda a, e: jnp.zeros_like(a) + jnp.asarray(e, a.dtype), value, neutral)

    def one(hop, state):
        return join(
            state,
            jax.tree.map(
                lambda a, own: lax.dynamic_index_in_dim(a, hop, 0, False).astype(own.dtype),
                gathered,
                value,
            ),
        )

    return lax.fori_loop(0, place, one, state)


def feature_map(values):
    widened = values.astype(jnp.float32)
    return jnp.where(widened > 0, widened + 1.0, jnp.exp(jnp.minimum(widened, 0.0))).astype(
        jnp.bfloat16
    )


def rms_norm(values, gain):
    widened = values.astype(jnp.float32)
    inverse = lax.rsqrt(jnp.mean(widened * widened, axis=-1, keepdims=True) + epsilon)
    return (widened * inverse * gain.astype(jnp.float32)).astype(jnp.bfloat16)


def attend_blocks(query_raw, key_feat, value_heads, state_sum, key_sum, block_size):
    length = query_raw.shape[0]
    heads_here = key_feat.shape[1]
    head_size = key_feat.shape[2]
    causal_mask = jnp.tril(jnp.ones((block_size, block_size), jnp.bool_))

    def into_blocks(array_in):
        return array_in.reshape(length // block_size, block_size, heads_here, head_size)

    def one_block(carry, inputs):
        running_state, running_keys = carry
        query_block, key_block, value_block = inputs
        query_block = feature_map(query_block)
        query_wide = query_block.astype(jnp.float32)
        scores = jnp.einsum(
            "bhi,chi->hbc", query_block, key_block, preferred_element_type=jnp.float32
        )
        scores = jnp.where(causal_mask[None], scores, 0.0)
        numerator = jnp.einsum(
            "hbc,chj->bhj", scores, value_block.astype(jnp.float32), precision=highest
        )
        numerator = numerator + jnp.einsum(
            "bhi,hij->bhj", query_wide, running_state, precision=highest
        )
        denominator = jnp.sum(scores, axis=2).T + jnp.einsum(
            "bhi,hi->bh", query_wide, running_keys, precision=highest
        )
        result = (numerator / denominator[:, :, None]).astype(jnp.bfloat16)
        running_state = running_state + jnp.einsum(
            "bhi,bhj->hij", key_block, value_block, preferred_element_type=jnp.float32
        )
        running_keys = running_keys + jnp.sum(key_block.astype(jnp.float32), axis=0)
        return ((running_state, running_keys), result)

    carry_out, outputs = lax.scan(
        one_block,
        (state_sum, key_sum),
        (into_blocks(query_raw), into_blocks(key_feat), into_blocks(value_heads)),
    )
    return outputs.reshape(length, heads_here * head_size)


def expert_grads(rows_in, scaled, gate_mat, up_mat, down_mat):
    gate_pre = jnp.dot(rows_in, gate_mat, preferred_element_type=jnp.float32)
    up_pre = jnp.dot(rows_in, up_mat, preferred_element_type=jnp.float32)
    sigmoid_gate = jax.nn.sigmoid(gate_pre)
    active = gate_pre * sigmoid_gate
    hidden_units = (active * up_pre).astype(jnp.bfloat16)
    grad_down = lax.dot_general(
        hidden_units, scaled, (((0,), (0,)), ((), ())), preferred_element_type=jnp.float32
    ).astype(jnp.bfloat16)
    grad_hidden = lax.dot_general(
        scaled, down_mat, (((1,), (1,)), ((), ())), preferred_element_type=jnp.float32
    )
    silu_slope = sigmoid_gate * (1.0 + gate_pre * (1.0 - sigmoid_gate))
    grad_pre_gate = (grad_hidden * up_pre * silu_slope).astype(jnp.bfloat16)
    grad_pre_up = (grad_hidden * active).astype(jnp.bfloat16)
    grad_gate = lax.dot_general(
        rows_in, grad_pre_gate, (((0,), (0,)), ((), ())), preferred_element_type=jnp.float32
    ).astype(jnp.bfloat16)
    grad_up = lax.dot_general(
        rows_in, grad_pre_up, (((0,), (0,)), ((), ())), preferred_element_type=jnp.float32
    ).astype(jnp.bfloat16)
    return (grad_gate, grad_up, grad_down)


def add_pair(earlier, later):
    return (earlier[0] + later[0], earlier[1] + later[1])


def on_device(
    queries,
    key_heads,
    value_heads,
    out_gain,
    out_weight,
    residual,
    norm_gain,
    routes,
    route_weights,
    cotangent,
    w_gate,
    w_up,
    w_down,
):
    length = queries.shape[0]
    heads_here = queries.shape[1] // HD
    block_size = min(512, length)
    key_feat = feature_map(key_heads.reshape(length, heads_here, HD))
    value_split = value_heads.reshape(length, heads_here, HD)
    span_state = jnp.einsum(
        "thi,thj->hij", key_feat, value_split, preferred_element_type=jnp.float32
    )
    span_keys = jnp.sum(key_feat.astype(jnp.float32), axis=0)
    start_state, start_keys = carried_in(
        (span_state, span_keys),
        "ctx",
        add_pair,
        (jnp.zeros_like(span_state), jnp.zeros_like(span_keys)),
    )
    attention = attend_blocks(
        queries.reshape(length, heads_here, HD),
        key_feat,
        value_split,
        start_state,
        start_keys,
        block_size,
    )
    tok_here = residual.shape[0]
    model_width = residual.shape[1]
    att_wide = attention.astype(jnp.float32)
    local_squares = jnp.sum(att_wide * att_wide, axis=1)
    total_squares = lax.psum(local_squares, "head")
    inv_rms = lax.rsqrt(total_squares / (HEADS * HD) + epsilon)
    normed = (att_wide * inv_rms[:, None] * out_gain.astype(jnp.float32)).astype(jnp.bfloat16)
    projected = lax.psum_scatter(
        jnp.dot(normed, out_weight, preferred_element_type=jnp.float32).astype(jnp.bfloat16),
        "head",
        scatter_dimension=0,
        tiled=True,
    ).astype(jnp.float32)
    hidden_out = (residual.astype(jnp.float32) + projected).astype(jnp.bfloat16)
    moe_in = rms_norm(hidden_out, norm_gain)
    per_block = tok_here * TOPK
    flat_routes = routes.reshape(per_block)
    onehot = (flat_routes[:, None] == jnp.arange(EXPERTS, dtype=jnp.int32)[None, :]).astype(
        jnp.int32
    )
    rank_in_block = jnp.sum(jnp.cumsum(onehot, axis=0) * onehot, axis=1) - 1
    local_experts = w_gate.shape[0]
    devices = lax.axis_size(("ctx", "head"))
    capacity = EXPERTS * 0 + max(2, tok_here * TOPK * 5 // (EXPERTS * 4))
    slot_rows = devices * capacity
    target = (
        flat_routes % local_experts * slot_rows
        + flat_routes // local_experts * capacity
        + rank_in_block
    )
    filler = (
        jnp.full((local_experts * slot_rows,), per_block, jnp.int32)
        .at[target]
        .set(jnp.arange(per_block, dtype=jnp.int32))
    )
    is_filled = filler < per_block
    safe_index = jnp.minimum(filler, per_block - 1)
    token_index = safe_index // TOPK
    rows_in = jnp.where(is_filled[:, None], moe_in[token_index], jnp.zeros((), jnp.bfloat16))
    weighted = route_weights.reshape(per_block)[safe_index][:, None] * cotangent[
        token_index
    ].astype(jnp.float32)
    scaled = jnp.where(is_filled[:, None], weighted, 0.0).astype(jnp.bfloat16)
    rows_in = rows_in.reshape(local_experts, slot_rows, model_width)
    scaled = scaled.reshape(local_experts, slot_rows, model_width)
    rows_in, scaled = (
        lax.all_to_all(rows_in, ("ctx", "head"), split_axis=1, concat_axis=1, tiled=True),
        lax.all_to_all(scaled, ("ctx", "head"), split_axis=1, concat_axis=1, tiled=True),
    )

    def per_expert(inputs):
        return expert_grads(inputs[0], inputs[1], inputs[2], inputs[3], inputs[4])

    grad_gate, grad_up, grad_down = lax.map(per_expert, (rows_in, scaled, w_gate, w_up, w_down))
    return (hidden_out, grad_gate, grad_up, grad_down)


def solution(mesh):
    in_specs = (
        P("ctx", "head"),
        P("ctx", "head"),
        P("ctx", "head"),
        P("head"),
        P("head", None),
        P(("ctx", "head"), None),
        P(),
        P(("ctx", "head"), None),
        P(("ctx", "head"), None),
        P(("ctx", "head"), None),
        P(("ctx", "head"), None, None),
        P(("ctx", "head"), None, None),
        P(("ctx", "head"), None, None),
    )
    out_specs = (
        P(("ctx", "head"), None),
        P(("ctx", "head"), None, None),
        P(("ctx", "head"), None, None),
        P(("ctx", "head"), None, None),
    )
    return jax.shard_map(
        on_device, mesh=mesh, in_specs=in_specs, out_specs=out_specs, check_vma=False
    )
```

profile of v0, /device:TPU:0, one launch (start us, length us, event | category | flops | bytes accessed | tf_op | source)
XLA Modules:
  0.0 465.5 jit_solution(17902966265471870790)
XLA Ops:
  11.6 2.2 reshape_reshape.7
  15.9 9.5 %all_gather.15 = bf16[4,4,128]{2,1,0:T(4,128)(2,1)S(1)} all-gather(bf16[1,4,128]{2,1,0:T(4,128)(2,1)S(1)} %bitcast.191), channel_id=1, replica_groups=mesh['ctx'=4,'head'=8] {'ctx'}, dimensions={0}, use_global_device_ids=true | all-gather | bytes 5120 | tf_op jit(solution)/shard_map/all_gather | solution.py:19
  27.4 10.2 %all-gather = bf16[16,128,128]{2,1,0:T(8,128)(2,1)S(1)} all-gather(bf16[4,128,128]{2,1,0:T(8,128)(2,1)S(1)} %convolution_convert_fusion.4), channel_id=2, replica_groups=mesh['ctx'=4,'head'=8] {'ctx'}, dimensions={0}, use_global_device_ids=true | all-gather | bytes 655360 | tf_op jit(solution)/shard_map/all_gather | solution.py:19
  37.7 19.9 %while.43 = (s32[]{:T(128)}, f32[4,128,128]{2,1,0:T(8,128)S(1)}, f32[4,128]{1,0:T(4,128)S(1)}, bf16[2,512,4,128]{1,3,2,0:T(8,128)(2,1)}, bf16[2,512,4,128]{3,2,1...) while((s32[]{:T(128)}, f32[4,128,128]{2,1,0:T(8,128)S(1)}, ...), condition=%wide.region_6.7_spmd.clone, body=%wide.region_3.6_spmd.clone.sunk | while | flops 2361458688 | bytes 30468284 | solution.py:83
  44.5 2.2 fusion.145
  54.5 2.2 fusion.145
  59.0 2.6 copy.68
  61.6 13.8 %psum.7 = f32[1024]{0:T(1024)S(1)} all-reduce(f32[1024]{0:T(1024)S(1)} %bitcast.190), channel_id=1, replica_groups=mesh['ctx'=4,'head'=8] {'head'}, use_global_device_ids=true, to_apply=%region_8.9 | all-reduce | flops 1024 | bytes 8192 | tf_op jit(solution)/shard_map/psum | solution.py:161
  75.4 6.0 %convolution_convert_fusion.3 = bf16[1024,2048]{1,0:T(8,128)(2,1)} fusion(bf16[512,2048]{1,0:T(8,128)(2,1)S(1)} %copy-done, f32[128,8,4,128]{3,2,1,0:T(4,128)} %bitcast.185, f32[512]{0:T(512)S(1)} %convert_element_type.116, f32[1024]{0:T(1024)S(1)} %add_rsqrt_fusion), kind=kOutput, calls=%fused_computation.86 | convolution fusion | flops 2151153664 | bytes 8394752 | tf_op jit(solution)/shard_map/dot_general | solution.py:165
  82.8 4.3 scatter_custom_fusion
  87.5 5.0 %gather_fusion.1 = f32[1280]{0:T(1024)S(1)} fusion(f32[1024]{0:T(1024)S(1)} %reshape.240, s32[2048]{0:T(1024)S(1)} %get-tuple-element.244), kind=kCustom, calls=%fused_computation.1 | custom fusion | bytes 15360 | tf_op jit(solution)/shard_map/gather | solution.py:196
  92.9 6.1 %gather_fusion.2 = bf16[1280,2048]{1,0:T(8,128)(2,1)} fusion(bf16[128,2048]{1,0:T(8,128)(2,1)S(1)} %copy-done.2, s32[2048]{0:T(1024)S(1)} %get-tuple-element.245), kind=kCustom, calls=%fused_computation.2 | custom fusion | bytes 10490880 | tf_op jit(solution)/shard_map/gather | solution.py:196
  99.0 4.0 convert.16
  102.9 7.6 %fusion.72 = bf16[4,320,2048]{2,0,1:T(4,128)(2,1)} fusion(f32[4,320,2048]{2,1,0:T(8,128)S(1)} %convert.16, f32[4,320]{0,1:T(8,128)S(1)} %copy.77, pred[4,320]{0,1:T(8,128)(4,1)S(1)} %copy.74), kind=kLoop, calls=%fused_computation.84 | loop fusion | flops 7864320 | bytes 15735040 | tf_op jit(solution)/shard_map/convert_element_type | solution.py:199
  110.5 3.7 all-to-all-start.1
  114.2 23.8 %reduce-scatter.2.cloned.1.call-done = bf16[128,2048]{1,0:T(8,128)(2,1)} async-done(((bf16[1024,2048]{1,0:T(8,128)(2,1)}), bf16[128,2048]{1,0:T(8,128)(2,1)}) %reduce-scatter.2.cloned.1.call-update) | async-done | bytes 524304 | tf_op jit(solution)/shard_map/reduce_scatter | solution.py:164
  139.5 6.1 %gather_fusion = bf16[1280,2048]{1,0:T(8,128)(2,1)} fusion(bf16[128,2048]{1,0:T(8,128)(2,1)S(1)} %fusion.80, s32[2048]{0:T(1024)S(1)} %get-tuple-element.245), kind=kCustom, calls=%fused_computation | custom fusion | bytes 10490880 | tf_op jit(solution)/shard_map/gather | solution.py:195
  145.6 9.1 %copy_select_fusion = bf16[4,320,2048]{2,0,1:T(4,128)(2,1)} fusion(bf16[4,320,2048]{2,1,0:T(8,128)(2,1)} %bitcast.180, pred[4,320]{0,1:T(8,128)(4,1)S(1)} %copy.74), kind=kLoop, calls=%fused_computation.85 | loop fusion | flops 2621440 | bytes 10487040 | tf_op jit(solution)/shard_map/jit(_where)/select_n | solution.py:195
  154.7 87.2 %all-to-all-done.1 = bf16[4,320,2048]{2,0,1:T(4,128)(2,1)} async-done(((bf16[4,320,2048]{2,0,1:T(4,128)(2,1)}), bf16[4,320,2048]{2,0,1:T(4,128)(2,1)}, u32[]{:S(2)}, u32[]{:S(2)}) %all-to-all-start.1) | async-done | bytes 5242912 | tf_op jit(solution)/shard_map/all_to_all | solution.py:204
  241.9 3.8 all-to-all-start
  245.8 7.7 %copy.80 = bf16[4,320,2048]{2,1,0:T(8,128)(2,1)} copy(bf16[4,320,2048]{2,0,1:T(4,128)(2,1)} %all-to-all-done.1) | data formatting | bytes 10485760 | tf_op jit(solution)/shard_map/while | solution.py:210
  253.4 109.6 %all-to-all-done = bf16[4,320,2048]{2,0,1:T(4,128)(2,1)} async-done(((bf16[4,320,2048]{2,0,1:T(4,128)(2,1)}), bf16[4,320,2048]{2,0,1:T(4,128)(2,1)}, u32[]{:S(2)}, u32[]{:S(2)}) %all-to-all-start) | async-done | bytes 5242912 | tf_op jit(solution)/shard_map/all_to_all | solution.py:203
  363.0 7.7 %copy.79 = bf16[4,320,2048]{2,1,0:T(8,128)(2,1)} copy(bf16[4,320,2048]{2,0,1:T(4,128)(2,1)} %all-to-all-done) | data formatting | bytes 10485760 | tf_op jit(solution)/shard_map/while | solution.py:210
  370.7 86.3 %while.42 = (s32[]{:T(128)}, bf16[4,2048,768]{2,1,0:T(8,128)(2,1)}, bf16[4,2048,768]{2,1,0:T(8,128)(2,1)}, bf16[4,768,2048]{2,1,0:T(8,128)(2,1)}, bf16[4,320,204...) while((s32[]{:T(128)}, bf16[4,2048,768]{2,1,0:T(8,128)(2,1)}, ...), condition=%wide.region_16.17_spmd, body=%wide.region_15.16_spmd.sunk | while | flops 6049923072 | bytes 73275576 | solution.py:210
  370.7 3.6 fusion.134
  374.6 3.6 fusion.136
  378.2 3.2 fusion.135
  381.4 3.6 bitcast_dynamic-update-slice_fusion.7
  385.1 3.7 bitcast_dynamic-update-slice_fusion.6
  388.8 3.6 bitcast_dynamic-update-slice_fusion.8
  392.3 3.6 fusion.134
  396.1 3.6 fusion.136
  399.8 3.2 fusion.135
  403.0 3.6 bitcast_dynamic-update-slice_fusion.7
  406.6 3.7 bitcast_dynamic-update-slice_fusion.6
  410.3 3.6 bitcast_dynamic-update-slice_fusion.8
  413.9 3.6 fusion.134
  417.7 3.6 fusion.136
  421.4 3.2 fusion.135
  424.6 3.6 bitcast_dynamic-update-slice_fusion.7
  428.2 3.7 bitcast_dynamic-update-slice_fusion.6
  431.9 3.6 bitcast_dynamic-update-slice_fusion.8
  435.5 3.6 fusion.134
  439.3 3.6 fusion.136
  443.0 3.2 fusion.135
  446.2 3.6 bitcast_dynamic-update-slice_fusion.7
  449.8 3.7 bitcast_dynamic-update-slice_fusion.6
  453.5 3.6 bitcast_dynamic-update-slice_fusion.8
  (126 shorter events, 31.4 us)
Async XLA Ops:
  7.2 68.3 %copy-start = (bf16[512,2048]{1,0:T(8,128)(2,1)S(1)}, bf16[512,2048]{1,0:T(8,128)(2,1)}, u32[]{:S(2)}) copy-start(bf16[512,2048]{1,0:T(8,128)(2,1)} %param.23) | copy-start | bytes 6291460
  7.2 130.8 %reduce-scatter.2.cloned.1.call-start = ((), (), s32[]{:S(2)}) async-start(), calls=%async_computation.3 | async-start | bytes 4718592 | tf_op jit(solution)/shard_map/reduce_scatter | solution.py:164
  37.6 24.0 %copy-start.12 = (bf16[512]{0:T(512)(128)(2,1)S(1)}, bf16[512]{0:T(512)(128)(2,1)}, u32[]{:S(2)}) copy-start(bf16[512]{0:T(512)(128)(2,1)} %param.22) | copy-start | bytes 3076
  40.0 3.5 copy-start.3
  42.4 2.1 copy-start.5
  46.7 1.0 copy-start.6
  50.0 3.5 copy-start.3
  52.3 2.1 copy-start.5
  56.6 1.0 copy-start.6
  75.4 6.1 %copy-start.9 = (s32[128,8]{0,1:T(8,128)S(1)}, s32[128,8]{0,1:T(8,128)}, u32[]{:S(2)}) copy-start(s32[128,8]{0,1:T(8,128)} %param.26) | copy-start | bytes 12292
  81.5 5.7 %copy-start.10 = (f32[128,8]{0,1:T(8,128)S(1)}, f32[128,8]{0,1:T(8,128)}, u32[]{:S(2)}) copy-start(f32[128,8]{0,1:T(8,128)} %param.27) | copy-start | bytes 12292
  82.3 10.6 %copy-start.2 = (bf16[128,2048]{1,0:T(8,128)(2,1)S(1)}, bf16[128,2048]{1,0:T(8,128)(2,1)}, u32[]{:S(2)}) copy-start(bf16[128,2048]{1,0:T(8,128)(2,1)} %param.28) | copy-start | bytes 1572868
  110.5 3.7 copy-start.11
  110.5 27.5 %copy-start.8 = (bf16[128,2048]{1,0:T(8,128)(2,1)S(1)}, bf16[128,2048]{1,0:T(8,128)(2,1)}, u32[]{:S(2)}) copy-start(bf16[128,2048]{1,0:T(8,128)(2,1)} %param.24) | copy-start | bytes 1572868
  110.5 131.4 %all-to-all-start.1 = ((bf16[4,320,2048]{2,0,1:T(4,128)(2,1)}), bf16[4,320,2048]{2,0,1:T(4,128)(2,1)}, u32[]{:S(2)}, u32[]{:S(2)}) async-start(bf16[4,320,2048]{2,0,1:T(4,128)(2,1)} %fusion.72), calls=%async_computation.2 | async-start | bytes 10485760 | tf_op jit(solution)/shard_map/all_to_all | solution.py:204
  139.3 6.3 %copy-start.7 = (bf16[128,2048]{1,0:T(8,128)(2,1)}, bf16[128,2048]{1,0:T(8,128)(2,1)S(1)}, u32[]{:S(2)}) copy-start(bf16[128,2048]{1,0:T(8,128)(2,1)S(1)} %get-tuple-element.235) | copy-start | bytes 1572868
  241.9 121.1 %all-to-all-start = ((bf16[4,320,2048]{2,0,1:T(4,128)(2,1)}), bf16[4,320,2048]{2,0,1:T(4,128)(2,1)}, u32[]{:S(2)}, u32[]{:S(2)}) async-start(bf16[4,320,2048]{2,0,1:T(4,128)(2,1)} %copy_select_fusion), calls=%async_computation.1 | async-start | bytes 10485760 | tf_op jit(solution)/shard_map/all_to_all | solution.py:203
  370.7 3.8 copy-start.4
  370.7 7.5 %slice-start = ((s8[5242880]{0:T(1024)(128)(4,1)}), s8[4194304]{0:T(1024)(128)(4,1)S(1)}, s32[]{:S(2)}) async-start(s8[5242880]{0:T(1024)(128)(4,1)} %bitcast.182), calls=%async_computation.4 | async-start | bytes 8388608 | tf_op jit(solution)/shard_map/while
  370.7 7.5 %slice-start.1 = ((s8[5242880]{0:T(1024)(128)(4,1)}), s8[1048576]{0:T(1024)(128)(4,1)S(1)}, s32[]{:S(2)}) async-start(s8[5242880]{0:T(1024)(128)(4,1)} %bitcast.182), calls=%async_computation.5 | async-start | bytes 2097152 | tf_op jit(solution)/shard_map/while
  392.3 3.8 copy-start.4
  392.3 7.5 %slice-start = ((s8[5242880]{0:T(1024)(128)(4,1)}), s8[4194304]{0:T(1024)(128)(4,1)S(1)}, s32[]{:S(2)}) async-start(s8[5242880]{0:T(1024)(128)(4,1)} %bitcast.182), calls=%async_computation.4 | async-start | bytes 8388608 | tf_op jit(solution)/shard_map/while
  392.3 7.5 %slice-start.1 = ((s8[5242880]{0:T(1024)(128)(4,1)}), s8[1048576]{0:T(1024)(128)(4,1)S(1)}, s32[]{:S(2)}) async-start(s8[5242880]{0:T(1024)(128)(4,1)} %bitcast.182), calls=%async_computation.5 | async-start | bytes 2097152 | tf_op jit(solution)/shard_map/while
  413.9 3.8 copy-start.4
  413.9 7.5 %slice-start = ((s8[5242880]{0:T(1024)(128)(4,1)}), s8[4194304]{0:T(1024)(128)(4,1)S(1)}, s32[]{:S(2)}) async-start(s8[5242880]{0:T(1024)(128)(4,1)} %bitcast.182), calls=%async_computation.4 | async-start | bytes 8388608 | tf_op jit(solution)/shard_map/while
  413.9 7.5 %slice-start.1 = ((s8[5242880]{0:T(1024)(128)(4,1)}), s8[1048576]{0:T(1024)(128)(4,1)S(1)}, s32[]{:S(2)}) async-start(s8[5242880]{0:T(1024)(128)(4,1)} %bitcast.182), calls=%async_computation.5 | async-start | bytes 2097152 | tf_op jit(solution)/shard_map/while
  435.5 3.8 copy-start.4
  435.5 7.5 %slice-start = ((s8[5242880]{0:T(1024)(128)(4,1)}), s8[4194304]{0:T(1024)(128)(4,1)S(1)}, s32[]{:S(2)}) async-start(s8[5242880]{0:T(1024)(128)(4,1)} %bitcast.182), calls=%async_computation.4 | async-start | bytes 8388608 | tf_op jit(solution)/shard_map/while
  435.5 7.5 %slice-start.1 = ((s8[5242880]{0:T(1024)(128)(4,1)}), s8[1048576]{0:T(1024)(128)(4,1)S(1)}, s32[]{:S(2)}) async-start(s8[5242880]{0:T(1024)(128)(4,1)} %bitcast.182), calls=%async_computation.5 | async-start | bytes 2097152 | tf_op jit(solution)/shard_map/while
  457.0 1.6 copy-start.1
Sparse Core Ops, SparseCore 0:
  81.6 56.3 reduce-scatter.1
where the time goes:
time: 467 us; the launch traced here: 465 us
  waiting for transfers between devices  221 us (47%)
  matrix products  103 us (22%)
  local copies, waits for them, and re-layouts  58.1 us (12%)
  blocking collectives  33.5 us (7%)
  other arithmetic  28.2 us (6%)
  between operations  14.3 us (3%)
  starting transfers between devices  7.57 us (2%)
    all_to_all x1, waiting for transfers between devices, on_device(): lax.all_to_all(rows_in, ('ctx', 'head'), split_axis=1, concat_axis=1, til...  110 us
    all_to_all x1, waiting for transfers between devices, on_device(): lax.all_to_all(scaled, ('ctx', 'head'), split_axis=1, concat_axis=1, tile...  87.2 us
    reduce_scatter x1, waiting for transfers between devices, on_device(): lax.psum_scatter(jnp.dot(normed, out_weight, preferred_element_type=jnp.f...  23.8 us
    all_gather x2, blocking collectives, carried_in(): lax.all_gather(a.astype(kind), axis)  19.7 us
    while x2, local copies, waits for them, and re-layouts, on_device(): lax.map(per_expert, (rows_in, scaled, w_gate, w_up, w_down))  15.4 us
    dot_general x4, matrix products, expert_grads(): lax.dot_general(rows_in, grad_pre_gate, (((0,), (0,)), ((), ())), preferr...  14.8 us
    dot_general x4, matrix products, expert_grads(): up_pre = jnp.dot(rows_in, up_mat, preferred_element_type=jnp.float32)  14.5 us
    dot_general x4, matrix products, expert_grads(): lax.dot_general(rows_in, grad_pre_up, (((0,), (0,)), ((), ())), preferred...  14.5 us
  transfers between devices with their start and end apart: 3, of which 3 were waited for; matrix products, arithmetic and copies ran while one was open for 11% of the time, Pallas kernels for 0%

commit v1 on v0

v1 whole, which is shorter than its diff:
```python
import functools

import jax
import jax.numpy as jnp
from jax import lax
from jax.experimental import pallas as pl
from jax.experimental.pallas import tpu as pltpu
from jax.sharding import PartitionSpec as P

HD = 128
EXPERTS = 128
TOPK = 8
SPAN = 8
MESH = pl.DeviceIdType.MESH
MIB = 1 << 20
epsilon = 1e-06
f32 = jnp.float32
bf16 = jnp.bfloat16


def feature_map(values):
    widened = values.astype(f32)
    return jnp.where(widened > 0, widened + 1.0, jnp.exp(jnp.minimum(widened, 0.0))).astype(bf16)


def rms_norm(values, gain):
    widened = values.astype(f32)
    inverse = lax.rsqrt(jnp.mean(widened * widened, axis=-1, keepdims=True) + epsilon)
    return (widened * inverse * gain.astype(f32)).astype(bf16)


def dot_tn(a, b):
    return lax.dot_general(a, b, (((0,), (0,)), ((), ())), preferred_element_type=f32)


def dot_nt(a, b):
    return lax.dot_general(a, b, (((1,), (1,)), ((), ())), preferred_element_type=f32)


def span_kernel(key_ref, value_ref, out_ref):
    feat = feature_map(key_ref[...])
    out_ref[0, :HD, :] = dot_tn(feat, value_ref[...]).astype(bf16)
    keys = jnp.sum(feat.astype(f32), axis=0, keepdims=True)
    row = lax.broadcasted_iota(jnp.int32, (16, HD), 0)
    out_ref[0, HD:, :] = jnp.where(row == 0, keys, 0.0).astype(bf16)


def span_sums(key_heads, value_heads):
    length, width = key_heads.shape
    heads = width // HD
    return pl.pallas_call(
        span_kernel,
        grid=(heads,),
        out_shape=jax.ShapeDtypeStruct((heads, HD + 16, HD), bf16),
        in_specs=[pl.BlockSpec((length, HD), lambda h: (0, h))] * 2,
        out_specs=pl.BlockSpec((1, HD + 16, HD), lambda h: (h, 0, 0)),
        compiler_params=pltpu.CompilerParams(vmem_limit_bytes=48 * MIB),
        name="span_sums",
    )(key_heads, value_heads)


def attend_kernel(block, place_ref, query_ref, key_ref, value_ref, sums_ref, gain_ref, out_ref, square_ref):
    head = pl.program_id(0)
    length = query_ref.shape[0]
    place = place_ref[0]
    state = jnp.zeros((HD, HD), f32)
    keys = jnp.zeros((1, HD), f32)
    for i in range(sums_ref.shape[0]):
        part = sums_ref[i, 0].astype(f32)
        state = state + jnp.where(i < place, part[:HD], 0.0)
        keys = keys + jnp.where(i < place, part[HD : HD + 1], 0.0)
    gain = gain_ref[...].astype(f32)
    row = lax.broadcasted_iota(jnp.int32, (block, block), 0)
    column = lax.broadcasted_iota(jnp.int32, (block, block), 1)
    for i in range(length // block):
        at = pl.ds(i * block, block)
        query = feature_map(query_ref[at, :])
        key = feature_map(key_ref[at, :])
        value = value_ref[at, :]
        scores = jnp.where(row >= column, dot_nt(query, key), 0.0)
        high = state.astype(bf16)
        low = (state - high.astype(f32)).astype(bf16)
        numerator = jnp.dot(scores.astype(bf16), value, preferred_element_type=f32)
        numerator = numerator + jnp.dot(query, high, preferred_element_type=f32)
        numerator = numerator + jnp.dot(query, low, preferred_element_type=f32)
        denominator = jnp.sum(scores, axis=1, keepdims=True)
        denominator = denominator + jnp.sum(query.astype(f32) * keys, axis=1, keepdims=True)
        result = (numerator / denominator).astype(bf16).astype(f32)
        out_ref[at, :] = (result * gain).astype(bf16)
        squares = result * result

        @pl.when(head == 0)
        def _():
            square_ref[at, :] = squares

        @pl.when(head != 0)
        def _():
            square_ref[at, :] = square_ref[at, :] + squares

        state = state + dot_tn(key, value)
        keys = keys + jnp.sum(key.astype(f32), axis=0, keepdims=True)


def attend(place, queries, key_heads, value_heads, sums, gain):
    length, width = queries.shape
    heads = width // HD
    block = 256 if length % 256 == 0 else length
    column = pl.BlockSpec((length, HD), lambda h: (0, h))
    return pl.pallas_call(
        functools.partial(attend_kernel, block),
        grid=(heads,),
        out_shape=[
            jax.ShapeDtypeStruct((length, width), bf16),
            jax.ShapeDtypeStruct((length, HD), f32),
        ],
        in_specs=[
            pl.BlockSpec(memory_space=pltpu.SMEM),
            column,
            column,
            column,
            pl.BlockSpec((sums.shape[0], 1, HD + 16, HD), lambda h: (0, h, 0, 0)),
            pl.BlockSpec((1, HD), lambda h: (0, h)),
        ],
        out_specs=[column, pl.BlockSpec((length, HD), lambda h: (0, 0))],
        compiler_params=pltpu.CompilerParams(vmem_limit_bytes=48 * MIB),
        name="attend",
    )(place, queries, key_heads, value_heads, sums, gain.reshape(1, width))


def gather_kernel(x_ref, out_ref, local_sem, zs, zr, ps, pr, ds, dr, ss, sr):
    rows = x_ref.shape[0]
    half = rows // 2
    i, h = lax.axis_index("ctx"), lax.axis_index("head")
    n_head = lax.axis_size("head")
    chips = n_head // 2
    k, c = h // 2, h % 2
    beside = (i // 2) * 2 + (1 - i % 2)
    above = (1 - i // 2) * 2 + i % 2
    across = 3 - i
    to_beside, to_above = (beside, h), (above, h)
    sibling = (i, k * 2 + 1 - c)
    right, left = (i, h + 2), (i, h - 2)

    barrier = pltpu.get_barrier_semaphore()
    for peer in (to_beside, to_above, sibling):
        pl.semaphore_signal(barrier, inc=1, device_id=peer, device_id_type=MESH)

    @pl.when(k > 0)
    def _():
        pl.semaphore_signal(barrier, inc=1, device_id=left, device_id_type=MESH)

    @pl.when(k < chips - 1)
    def _():
        pl.semaphore_signal(barrier, inc=1, device_id=right, device_id_type=MESH)

    peers = 3 + (k + chips - 1) // chips + (2 * chips - 2 - k) // chips
    pl.semaphore_wait(barrier, peers)

    def span(ctx, chip, part=None):
        start = ((ctx * n_head) + chip * 2 + c) * rows
        if part is None:
            return pl.ds(pl.multiple_of(start, 16), rows)
        return pl.ds(pl.multiple_of(start + part * half, 16), half)

    def send(src, at, send_sem, recv_sem, peer):
        return pltpu.make_async_remote_copy(
            src_ref=src, dst_ref=out_ref.at[at], send_sem=send_sem, recv_sem=recv_sem,
            device_id=peer, device_id_type=MESH,
        )

    def here(at):
        return out_ref.at[at]

    groups = 1 + 2 * (chips - 1)

    def chip_of(g):
        if g == 0:
            return k
        return k - 1 - (g - 1) // 2 if g % 2 == 1 else k + 1 + (g - 2) // 2

    def valid(g):
        if g == 0:
            return None
        return chip_of(g) >= 0 if g % 2 == 1 else chip_of(g) < chips

    def when(g, body):
        if valid(g) is None:
            body()
        else:
            pl.when(valid(g))(body)

    def plane(g):
        at = span(i, chip_of(g))
        src = x_ref if g == 0 else here(at)
        return [
            send(src, at, ps.at[g, 0], pr.at[g, 0], to_beside),
            send(src, at, ps.at[g, 1], pr.at[g, 1], to_above),
            send(src, at, ss.at[g, 0], sr.at[g, 0], sibling),
        ]

    def diagonal(g):
        chip = chip_of(g)
        top, bottom = span(beside, chip, 0), span(above, chip, 1)
        whole_b, whole_a = span(beside, chip), span(above, chip)
        return [
            send(here(top), top, ds.at[g, 0], dr.at[g, 0], to_above),
            send(here(bottom), bottom, ds.at[g, 1], dr.at[g, 1], to_beside),
            send(here(whole_b), whole_b, ss.at[g, 1], sr.at[g, 1], sibling),
            send(here(whole_a), whole_a, ss.at[g, 2], sr.at[g, 2], sibling),
        ]

    def last(g):
        at = span(across, chip_of(g))
        return [send(here(at), at, ss.at[g, 3], sr.at[g, 3], sibling)]

    def onward(g):
        at = span(i, chip_of(g))
        src = x_ref if g == 0 else here(at)
        copies = []
        if g == 0:
            copies.append((k < chips - 1, send(src, at, zs.at[1], zr.at[1], right)))
            copies.append((k > 0, send(src, at, zs.at[2], zr.at[2], left)))
        elif g + 2 < groups:
            go = k < chips - 1 if g % 2 == 1 else k > 0
            copies.append((go, send(src, at, zs.at[g + 2], zr.at[g + 2], right if g % 2 == 1 else left)))
        return copies

    def begin(g):
        def body():
            if g > 0:
                at = span(i, chip_of(g))
                send(here(at), at, zs.at[g], zr.at[g], left if g % 2 == 1 else right).wait_recv()
            for go, copy in onward(g):
                pl.when(go)(copy.start)
            for copy in plane(g):
                copy.start()

        when(g, body)

    def middle(g):
        def body():
            chip = chip_of(g)
            at = span(beside, chip)
            send(here(at), at, ps.at[g, 0], pr.at[g, 0], to_beside).wait_recv()
            at = span(above, chip)
            send(here(at), at, ps.at[g, 1], pr.at[g, 1], to_above).wait_recv()
            for copy in diagonal(g):
                copy.start()

        when(g, body)

    def finish(g):
        def body():
            chip = chip_of(g)
            at = span(across, chip, 0)
            send(here(at), at, ds.at[g, 0], dr.at[g, 0], to_above).wait_recv()
            at = span(across, chip, 1)
            send(here(at), at, ds.at[g, 1], dr.at[g, 1], to_beside).wait_recv()
            for copy in last(g):
                copy.start()

        when(g, body)

    def drain(g):
        def body():
            for copy in plane(g) + diagonal(g) + last(g):
                copy.wait_send()
            for go, copy in onward(g):
                pl.when(go)(copy.wait_send)
            chip = chip_of(g)
            for j, ctx in enumerate((i, beside, above, across)):
                start = ((ctx * n_head) + chip * 2 + 1 - c) * rows
                at = pl.ds(pl.multiple_of(start, 16), rows)
                send(here(at), at, ss.at[g, j], sr.at[g, j], sibling).wait_recv()

        when(g, body)

    own = pltpu.make_async_copy(x_ref, here(span(i, k)), local_sem)
    own.start()
    stages = [[0]] + [[1 + 2 * s, 2 + 2 * s] for s in range(chips - 1)]
    for s in range(len(stages) + 2):
        for step, late in ((begin, 0), (middle, 1), (finish, 2)):
            if 0 <= s - late < len(stages):
                for g in stages[s - late]:
                    step(g)
    own.wait()
    for g in range(groups):
        drain(g)


def gather_rows(x, devices, chips):
    groups = 1 + 2 * (chips - 1)
    dma = pltpu.SemaphoreType.DMA
    return pl.pallas_call(
        gather_kernel,
        out_shape=jax.ShapeDtypeStruct((devices * x.shape[0], x.shape[1]), x.dtype),
        in_specs=[pl.BlockSpec(memory_space=pl.ANY)],
        out_specs=pl.BlockSpec(memory_space=pl.ANY),
        scratch_shapes=[
            dma, dma((groups,)), dma((groups,)), dma((groups, 2)), dma((groups, 2)),
            dma((groups, 2)), dma((groups, 2)), dma((groups, 4)), dma((groups, 4)),
        ],
        compiler_params=pltpu.CompilerParams(collective_id=0, has_side_effects=True),
        name="gather_rows",
    )(x)


def pick_kernel(scale, target_ref, weight_ref, x_ref, out_ref):
    experts, slots = out_ref.shape[0], out_ref.shape[1]
    tokens = x_ref.shape[0]
    slot = lax.broadcasted_iota(jnp.int32, (slots, tokens), 0)
    for e in range(experts):
        chosen = slot == target_ref[e : e + 1, :]
        rows = jnp.dot(chosen.astype(f32).astype(bf16), x_ref[...], preferred_element_type=f32)
        if scale:
            weights = jnp.sum(jnp.where(chosen, weight_ref[e : e + 1, :], 0.0), axis=1, keepdims=True)
            rows = rows * weights
        out_ref[e] = rows.astype(bf16)


def pick(target, weight, x, capacity, block_rows, scale):
    experts, tokens = target.shape
    span = SPAN * block_rows
    slots = SPAN * capacity
    steps = tokens // span
    meta = pl.BlockSpec((experts, span), lambda s: (0, s))
    return pl.pallas_call(
        functools.partial(pick_kernel, scale),
        grid=(steps,),
        out_shape=jax.ShapeDtypeStruct((experts, steps * slots, x.shape[1]), bf16),
        in_specs=[meta, meta, pl.BlockSpec((span, x.shape[1]), lambda s: (s, 0))],
        out_specs=pl.BlockSpec((experts, slots, x.shape[1]), lambda s: (0, s, 0)),
        compiler_params=pltpu.CompilerParams(vmem_limit_bytes=56 * MIB),
        cost_estimate=pl.CostEstimate(
            flops=2 * experts * slots * tokens * x.shape[1],
            bytes_accessed=2 * x.size + 2 * experts * steps * slots * x.shape[1],
            transcendentals=0,
        ),
        name="pick_scaled" if scale else "pick_rows",
    )(target, weight, x)


def expert_kernel(rows_ref, scaled_ref, gate_ref, up_ref, down_ref, dgate_ref, dup_ref, ddown_ref, turned):
    @pl.when(pl.program_id(1) == 0)
    def _():
        turned[...] = rows_ref[0].T

    rows, scaled = rows_ref[0], scaled_ref[0]
    gate_pre = jnp.dot(rows, gate_ref[0], preferred_element_type=f32)
    up_pre = jnp.dot(rows, up_ref[0], preferred_element_type=f32)
    grad_hidden = dot_nt(scaled, down_ref[0])
    sigmoid_gate = jax.nn.sigmoid(gate_pre)
    active = gate_pre * sigmoid_gate
    hidden_units = (active * up_pre).astype(bf16)
    silu_slope = sigmoid_gate * (1.0 + gate_pre * (1.0 - sigmoid_gate))
    grad_pre_gate = (grad_hidden * up_pre * silu_slope).astype(bf16)
    grad_pre_up = (grad_hidden * active).astype(bf16)
    ddown_ref[0] = dot_tn(hidden_units, scaled).astype(bf16)
    dgate_ref[0] = jnp.dot(turned[...], grad_pre_gate, preferred_element_type=f32).astype(bf16)
    dup_ref[0] = jnp.dot(turned[...], grad_pre_up, preferred_element_type=f32).astype(bf16)


def expert_grads(rows_in, scaled, w_gate, w_up, w_down):
    experts, width, units = w_gate.shape
    slots = rows_in.shape[1]
    tile = 256 if units % 256 == 0 else units
    token = pl.BlockSpec((1, slots, width), lambda e, f: (e, 0, 0))
    wide = pl.BlockSpec((1, width, tile), lambda e, f: (e, 0, f))
    tall = pl.BlockSpec((1, tile, width), lambda e, f: (e, f, 0))
    return pl.pallas_call(
        expert_kernel,
        grid=(experts, units // tile),
        out_shape=[
            jax.ShapeDtypeStruct(w_gate.shape, bf16),
            jax.ShapeDtypeStruct(w_up.shape, bf16),
            jax.ShapeDtypeStruct(w_down.shape, bf16),
        ],
        in_specs=[token, token, wide, wide, tall],
        out_specs=[wide, wide, tall],
        scratch_shapes=[pltpu.VMEM((width, slots), bf16)],
        compiler_params=pltpu.CompilerParams(vmem_limit_bytes=58 * MIB),
        cost_estimate=pl.CostEstimate(
            flops=12 * experts * slots * width * units,
            bytes_accessed=12 * experts * width * units + 4 * experts * slots * width,
            transcendentals=experts * slots * units,
        ),
        name="expert_grads",
    )(rows_in, scaled, w_gate, w_up, w_down)


def exchange_slots(moe_in, routes, route_weights, cotangent, local_experts, capacity, devices):
    tok_here, width = moe_in.shape
    per_block = tok_here * TOPK
    flat = routes.reshape(per_block)
    onehot = (flat[:, None] == jnp.arange(EXPERTS, dtype=jnp.int32)[None, :]).astype(jnp.int32)
    rank = jnp.sum(jnp.cumsum(onehot, axis=0) * onehot, axis=1) - 1
    slot_rows = devices * capacity
    target = flat % local_experts * slot_rows + flat // local_experts * capacity + rank
    filler = jnp.full((local_experts * slot_rows,), per_block, jnp.int32)
    filler = filler.at[target].set(jnp.arange(per_block, dtype=jnp.int32))
    is_filled = (filler < per_block)[:, None]
    index = jnp.minimum(filler, per_block - 1)
    token = index // TOPK
    rows_in = jnp.where(is_filled, moe_in[token], jnp.zeros((), bf16))
    weighted = route_weights.reshape(per_block)[index][:, None] * cotangent[token].astype(f32)
    scaled = jnp.where(is_filled, weighted, 0.0).astype(bf16)
    return tuple(
        lax.all_to_all(
            a.reshape(local_experts, slot_rows, width), ("ctx", "head"), split_axis=1, concat_axis=1, tiled=True
        )
        for a in (rows_in, scaled)
    )


def on_device(
    queries, key_heads, value_heads, out_gain, out_weight, residual, norm_gain,
    routes, route_weights, cotangent, w_gate, w_up, w_down,
):
    both = ("ctx", "head")
    n_ctx, n_head = lax.axis_size("ctx"), lax.axis_size("head")
    devices = n_ctx * n_head
    tok_here, width = residual.shape
    local_experts = w_gate.shape[0]
    capacity = max(2, tok_here * TOPK * 5 // (EXPERTS * 4))
    whole = (
        n_ctx == 4 and n_head % 2 == 0 and devices % SPAN == 0
        and devices * tok_here <= 4 * local_experts * devices * capacity
    )

    if whole:
        with jax.named_scope("gather_cotangent"):
            cot_all = lax.all_gather(cotangent, both, axis=0, tiled=True)
            meta = jnp.concatenate([routes.astype(f32), route_weights], axis=1).T
            meta = lax.all_gather(meta, both, axis=0)

    sums = lax.all_gather(span_sums(key_heads, value_heads), "ctx")
    place = lax.axis_index("ctx").astype(jnp.int32).reshape(1)
    scaled_att, squares = attend(place, queries, key_heads, value_heads, sums, out_gain)
    partial = jnp.dot(scaled_att, out_weight, preferred_element_type=f32).astype(bf16)
    projected = lax.psum_scatter(partial, "head", scatter_dimension=0, tiled=True).astype(f32)
    total = lax.psum_scatter(jnp.sum(squares, axis=1), "head", scatter_dimension=0, tiled=True)
    inv_rms = lax.rsqrt(total / (queries.shape[1] * n_head) + epsilon)
    hidden_out = (residual.astype(f32) + projected * inv_rms[:, None]).astype(bf16)
    moe_in = rms_norm(hidden_out, norm_gain)

    if whole:
        with jax.named_scope("slots"):
            mine = (lax.axis_index(both) * local_experts).astype(f32) + jnp.arange(local_experts, dtype=f32)
            named = meta[None, :, :TOPK, :] == mine[:, None, None, None]
            weight = jnp.sum(jnp.where(named, meta[None, :, TOPK:, :], 0.0), axis=2)
            member = jnp.any(named, axis=2)
            before = jnp.triu(jnp.ones((tok_here, tok_here), bf16), 1)
            rank = jnp.dot(member.astype(bf16), before, preferred_element_type=f32).astype(jnp.int32)
            turn = (jnp.arange(devices, dtype=jnp.int32) % SPAN * capacity)[None, :, None]
            target = jnp.where(member, rank + turn, -1).reshape(local_experts, devices * tok_here)
            weight = weight.reshape(local_experts, devices * tok_here)
        scaled = pick(target, weight, cot_all, capacity, tok_here, True)
        rows_all = gather_rows(moe_in, devices, n_head // 2)
        rows_in = pick(target, weight, rows_all, capacity, tok_here, False)
    else:
        rows_in, scaled = exchange_slots(
            moe_in, routes, route_weights, cotangent, local_experts, capacity, devices
        )
    grad_gate, grad_up, grad_down = expert_grads(rows_in, scaled, w_gate, w_up, w_down)
    return (hidden_out, grad_gate, grad_up, grad_down)


def solution(mesh):
    tokens = P(("ctx", "head"), None)
    experts = P(("ctx", "head"), None, None)
    in_specs = (
        P("ctx", "head"), P("ctx", "head"), P("ctx", "head"), P("head"), P("head", None),
        tokens, P(), tokens, tokens, tokens, experts, experts, experts,
    )
    out_specs = (tokens, experts, experts, experts)
    return jax.shard_map(on_device, mesh=mesh, in_specs=in_specs, out_specs=out_specs, check_vma=False)
```

time: 467 us -> 307 us (0.66)
  waiting for transfers between devices: 221 us -> 14.9 us
  Pallas kernels: 0 us -> 191 us
  matrix products: 103 us -> 4.5 us
  local copies, waits for them, and re-layouts: 58.1 us -> 6.5 us
  blocking collectives: 33.5 us -> 70.5 us
  other arithmetic: 28.2 us -> 3.18 us
  starting transfers between devices: 7.57 us -> 0.08 us
    all_to_all x2 -> x0, waiting for transfers between devices: 197 us -> none  [the longest x1 110 us: on_device(): lax.all_to_all(rows_in, ('ctx', 'head'), split_axis=1, concat_axis=1, til...]
    pallas_call x0 -> x6, Pallas kernels: none -> 191 us  [the longest x1 105 us: gather_rows(): pl.pallas_call(gather_kernel, out_shape=jax.ShapeDtypeStruct((devices * x...]
    dot_general x36 -> x2, matrix products: 103 us -> 4.5 us  [the longest x1 4.36 us: on_device(): jnp.dot(scaled_att, out_weight, preferred_element_type=f32).astype(bf16)]
    all_gather x2, blocking collectives: 19.7 us -> 55.6 us  [the longest x1 43.8 us: on_device(): meta = lax.all_gather(meta, both, axis=0)]
    while x38 -> x0, local copies, waits for them, and re-layouts: 18.2 us -> none  [the longest x2 15.4 us: on_device(): lax.map(per_expert, (rows_in, scaled, w_gate, w_up, w_down))]
    gather x3 -> x0, local copies, waits for them, and re-layouts: 17.1 us -> none  [the longest x1 6.08 us: on_device(): cotangent[token_index].astype(jnp.float32)]
    unnamed x0 -> x1, blocking collectives: none -> 14.9 us
    psum x1 -> x0, blocking collectives: 13.8 us -> none  [on_device(): total_squares = lax.psum(local_squares, 'head')]
  transfers between devices with their start and end apart: 3 -> 2, of which waited for: 3 -> 1; matrix products, arithmetic and copies ran while one was open for 11% -> 2% of each run, Pallas kernels for 0% -> 39%
where the time goes in v1:
time: 307 us
  Pallas kernels  191 us (62%)
  blocking collectives  70.5 us (23%)
  between operations  16.3 us (5%)
  waiting for transfers between devices  14.9 us (5%)
  local copies, waits for them, and re-layouts  6.5 us (2%)
  matrix products  4.5 us (1%)
  other arithmetic  3.18 us (1%)
    pallas_call x1, Pallas kernels, gather_rows(): pl.pallas_call(gather_kernel, out_shape=jax.ShapeDtypeStruct((devices * x...  105 us
    pallas_call x1, Pallas kernels, expert_grads(): pl.pallas_call(expert_kernel, grid=(experts, units // tile), out_shape=[j...  44.4 us
    all_gather x1, blocking collectives, on_device(): meta = lax.all_gather(meta, both, axis=0)  43.8 us
    pallas_call x2, Pallas kernels, pick(): pl.pallas_call(functools.partial(pick_kernel, scale), grid=(steps,), out_...  31.2 us
    unnamed x1, blocking collectives  14.9 us
    reduce_scatter x1, waiting for transfers between devices, on_device(): lax.psum_scatter(partial, 'head', scatter_dimension=0, tiled=True)  14.4 us
    all_gather x1, blocking collectives, on_device(): sums = lax.all_gather(span_sums(key_heads, value_heads), 'ctx')  11.8 us
    pallas_call x1, Pallas kernels, attend(): pl.pallas_call(functools.partial(attend_kernel, block), grid=(heads,), ou...  8 us
  transfers between devices with their start and end apart: 2, of which 1 were waited for; matrix products, arithmetic and copies ran while one was open for 2% of the time, Pallas kernels for 39%

profile of v1, /device:TPU:0, one launch (start us, length us, event | category | flops | bytes accessed | tf_op | source)
XLA Modules:
  0.0 306.8 jit_solution(4935289860258564645)
XLA Ops:
  8.0 0.0 copy-start
  8.0 0.0 reduce-scatter.2.cloned.1.call-start
  8.1 0.8 reshape.47.gain_ref
  8.9 0.0 copy-start.2
  8.9 1.2 copy-done.2
  10.1 0.0 copy-start.3
  10.1 1.2 copy-done.3
  11.3 1.8 span_sums.1
  13.2 11.8 %all-gather = bf16[16,144,128]{2,1,0:T(8,128)(2,1)S(1)} all-gather(bf16[4,144,128]{2,1,0:T(8,128)(2,1)S(1)} %span_sums.1), channel_id=2, replica_groups=mesh['ctx'=4,'head'=8] {'ctx'}, dimensions={0}, use_global_device_ids=true | all-gather | bytes 737280 | tf_op jit(solution)/shard_map/all_gather | solution.py:436
  24.9 0.0 copy-start.4
  24.9 1.2 copy-done.4
  26.2 8.0 %attend.1 = (bf16[1024,512]{1,0:T(8,128)(2,1)S(1)}, f32[1024,128]{1,0:T(8,128)S(1)}) custom-call(s32[1]{0:T(128)} %bitcast.place_ref, bf16[1024,512]{1,0:T(8,128)(2,1)S(1)} %copy-done.4, bf16[1024,512]{1,0:T(8,128)(2,1)S(1)} %copy-done.2, bf16[1024,512]{1,0:T(8,128)(2,1)S(1)} %copy-done.3, bf16[4,4,144,128]{3,2,1,0:T(8,128)(2,1)S(1)} %bitcast.21, ...), custom_call_target="tpu_custom_call" | custom-call | tf_op jit(solution)/shard_map/attend/pallas_call | solution.py:109
  34.2 0.0 copy-start.8
  34.2 0.0 copy-start.7
  34.2 0.0 copy-start.9
  34.2 0.0 copy-done
  34.2 0.0 copy-start.10
  34.2 0.0 copy-start.6
  34.2 4.4 %convolution_convert_fusion = bf16[1024,2048]{1,0:T(8,128)(2,1)} fusion(bf16[1024,512]{1,0:T(8,128)(2,1)S(1)} %get-tuple-element.9, bf16[512,2048]{1,0:T(8,128)(2,1)S(1)} %copy-done), kind=kOutput, calls=%fused_computation | convolution fusion | flops 2149580800 | bytes 7340032 | tf_op jit(solution)/shard_map/dot_general | solution.py:439
  38.6 0.0 reduce-scatter.2.cloned.1.call-update
  38.6 0.0 all-gather.4.cloned.1.call-start
  38.7 0.5 all-gather.4.cloned.1.call-update
  39.2 0.0 copy-done.8
  39.2 0.0 copy-done.7
  39.3 0.0 copy-done.9
  39.3 43.8 %all-gather.1 = f32[512,128]{1,0:T(8,128)S(1)} all-gather(f32[16,128]{1,0:T(8,128)S(1)} %maximum_bitcast_fusion), channel_id=3, replica_groups=mesh['ctx'=4,'head'=8] {'ctx','head'}, dimensions={0}, use_global_device_ids=true | all-gather | bytes 270336 | tf_op jit(solution)/shard_map/gather_cotangent/all_gather | solution.py:434
  83.1 0.2 fusion.6
  83.4 0.7 copy.21
  84.0 0.2 compare_reduce_fusion
  84.3 0.1 fusion.2
  84.4 0.7 copy.22
  85.1 0.0 copy-done.10
  85.1 0.6 dynamic-slice
  86.3 0.2 reduce_sum.27
  86.5 14.9 %all-reduce = f32[1024]{0:T(1024)S(1)} all-reduce(f32[1024]{0:T(1024)S(1)} %reduce_sum.27), channel_id=5, replica_groups=mesh['ctx'=4,'head'=8] {'head'}, use_global_device_ids=true, to_apply=%region_2.0.clone | all-reduce | flops 1024 | bytes 8192
  101.4 0.1 fusion.14
  101.5 14.4 %reduce-scatter.2.cloned.1.call-done = bf16[128,2048]{1,0:T(8,128)(2,1)} async-done(((bf16[1024,2048]{1,0:T(8,128)(2,1)}), bf16[128,2048]{1,0:T(8,128)(2,1)}) %reduce-scatter.2.cloned.1.call-update) | async-done | bytes 524304 | tf_op jit(solution)/shard_map/reduce_scatter | solution.py:440
  115.9 0.0 copy-done.6
  115.9 1.4 fusion.3
  117.3 0.0 copy-start.5
  117.3 1.0 fusion.5.x_ref
  118.3 105.3 %gather_rows.1.x_ref = bf16[4096,2048]{1,0:T(8,128)(2,1)} custom-call(bf16[128,2048]{1,0:T(8,128)(2,1)} %fusion.5.x_ref), custom_call_target="tpu_custom_call" | custom-call | tf_op jit(solution)/shard_map/gather_rows/pallas_call | solution.py:294
  223.6 0.0 copy-done.5
  223.6 15.6 %pick_rows.1.rows_ref = bf16[4,320,2048]{2,1,0:T(8,128)(2,1)} custom-call(s32[4,4096]{1,0:T(4,128)} %bitcast.25, f32[4,4096]{1,0:T(4,128)} %bitcast.23, bf16[4096,2048]{1,0:T(8,128)(2,1)} %gather_rows.1.x_ref), custom_call_target="tpu_custom_call" | custom-call | flops 5368709120 | bytes 22020096 | tf_op jit(solution)/shard_map/pick_rows/pallas_call | solution.py:327
  239.2 0.0 all-gather.4.cloned.1.call-done.x_ref
  239.2 15.6 %pick_scaled.1.scaled_ref = bf16[4,320,2048]{2,1,0:T(8,128)(2,1)} custom-call(s32[4,4096]{1,0:T(4,128)} %bitcast.26, f32[4,4096]{1,0:T(4,128)} %bitcast.24, bf16[4096,2048]{1,0:T(8,128)(2,1)} %all-gather.4.cloned.1.call-done.x_ref), custom_call_target="tpu_custom_call" | custom-call | flops 5368709120 | bytes 22020096 | tf_op jit(solution)/shard_map/pick_scaled/pallas_call | solution.py:327
  254.9 44.4 %expert_grads.1 = (bf16[4,2048,768]{2,1,0:T(8,128)(2,1)}, bf16[4,2048,768]{2,1,0:T(8,128)(2,1)}, bf16[4,768,2048]{2,1,0:T(8,128)(2,1)}) custom-call(bf16[4,320,2048]{2,1,0:T(8,128)(2,1)} %pick_rows.1.rows_ref, bf16[4,320,2048]{2,1,0:T(8,128)(2,1)} %pick_scaled.1.scaled_ref, bf16[4,2048,768]{2,1,0:T(8,128)(2,1)} %gate_ref.1, bf16[4,2048,768]{2,1,0:T(8,128)(2,1)} %up_ref.1, ...), custom_call_target="tpu_custom_call" | custom-call | flops 24159191040 | bytes 85983232 | tf_op jit(solution)/shard_map/expert_grads/pallas_call | solution.py:370
  299.3 0.0 copy-done.1
  (8 shorter events, 0.0 us)
Async XLA Ops:
  8.0 26.2 %copy-start = (bf16[512,2048]{1,0:T(8,128)(2,1)S(1)}, bf16[512,2048]{1,0:T(8,128)(2,1)}, u32[]{:S(2)}) copy-start(bf16[512,2048]{1,0:T(8,128)(2,1)} %param.17) | copy-start | bytes 6291460
  8.0 107.8 %reduce-scatter.2.cloned.1.call-start = ((), (), s32[]{:S(2)}) async-start(), calls=%async_computation.1 | async-start | bytes 4718592 | tf_op jit(solution)/shard_map/reduce_scatter | solution.py:440
  8.9 1.2 copy-start.2
  10.1 1.2 copy-start.3
  24.9 1.2 copy-start.4
  34.2 5.1 %copy-start.8 = (s32[128,8]{0,1:T(8,128)S(1)}, s32[128,8]{0,1:T(8,128)}, u32[]{:S(2)}) copy-start(s32[128,8]{0,1:T(8,128)} %param.20) | copy-start | bytes 12292
  34.2 5.1 %copy-start.7 = (bf16[2048]{0:T(1024)(128)(2,1)S(1)}, bf16[2048]{0:T(1024)(128)(2,1)}, u32[]{:S(2)}) copy-start(bf16[2048]{0:T(1024)(128)(2,1)} %param.19) | copy-start | bytes 12292
  34.2 5.1 %copy-start.9 = (f32[128,8]{0,1:T(8,128)S(1)}, f32[128,8]{0,1:T(8,128)}, u32[]{:S(2)}) copy-start(f32[128,8]{0,1:T(8,128)} %param.21) | copy-start | bytes 12292
  34.2 50.9 %copy-start.10 = (u32[32]{0:T(128)S(1)}, u32[32]{0:T(128)}, u32[]{:S(2)}) copy-start(u32[32]{0:T(128)} %constant.53) | copy-start | bytes 388
  34.2 81.6 %copy-start.6 = (bf16[128,2048]{1,0:T(8,128)(2,1)S(1)}, bf16[128,2048]{1,0:T(8,128)(2,1)}, u32[]{:S(2)}) copy-start(bf16[128,2048]{1,0:T(8,128)(2,1)} %param.18) | copy-start | bytes 1572868
  38.6 200.6 %all-gather.4.cloned.1.call-start = ((), (), s32[]{:S(2)}) async-start(), calls=%async_computation.2 | async-start | bytes 17301504 | tf_op jit(solution)/shard_map/gather_cotangent/all_gather | solution.py:432
  117.3 106.3 %copy-start.5 = (bf16[128,2048]{1,0:T(8,128)(2,1)}, bf16[128,2048]{1,0:T(8,128)(2,1)S(1)}, u32[]{:S(2)}) copy-start(bf16[128,2048]{1,0:T(8,128)(2,1)S(1)} %get-tuple-element.15) | copy-start | bytes 1572868
  254.9 44.4 %copy-start.1 = (bf16[512,2048]{1,0:T(8,128)(2,1)S(1)}, bf16[512,2048]{1,0:T(8,128)(2,1)}, u32[]{:S(2)}) copy-start(bf16[512,2048]{1,0:T(8,128)(2,1)} %param.17) | copy-start | bytes 6291460
Sparse Core Ops, SparseCore 0:
  38.7 77.0 reduce-scatter.1
Sparse Core Ops, SparseCore 1:
  42.1 167.1 all-gather.3

commit v2 on v1

--- a/solution.py
+++ b/solution.py
@@ -127,7 +127,7 @@
     )(place, queries, key_heads, value_heads, sums, gain.reshape(1, width))
 
 
-def gather_kernel(x_ref, out_ref, local_sem, zs, zr, ps, pr, ds, dr, ss, sr):
+def gather_kernel(x_ref, out_ref, local_sem, zs, zr, ps, pr, ds, dr, ss, sr, first=None, work=()):
     rows = x_ref.shape[0]
     half = rows // 2
     i, h = lax.axis_index("ctx"), lax.axis_index("head")
@@ -142,7 +142,8 @@
     right, left = (i, h + 2), (i, h - 2)
 
     barrier = pltpu.get_barrier_semaphore()
-    for peer in (to_beside, to_above, sibling):
+    greeted = [to_beside, to_above, sibling] + ([(across, h)] if first else [])
+    for peer in greeted:
         pl.semaphore_signal(barrier, inc=1, device_id=peer, device_id_type=MESH)
 
     @pl.when(k > 0)
@@ -153,7 +154,7 @@
     def _():
         pl.semaphore_signal(barrier, inc=1, device_id=right, device_id_type=MESH)
 
-    peers = 3 + (k + chips - 1) // chips + (2 * chips - 2 - k) // chips
+    peers = len(greeted) + (k + chips - 1) // chips + (2 * chips - 2 - k) // chips
     pl.semaphore_wait(barrier, peers)
 
     def span(ctx, chip, part=None):
@@ -275,6 +276,8 @@
 
         when(g, body)
 
+    if first:
+        first(i, (to_beside, to_above, (across, h)))
     own = pltpu.make_async_copy(x_ref, here(span(i, k)), local_sem)
     own.start()
     stages = [[0]] + [[1 + 2 * s, 2 + 2 * s] for s in range(chips - 1)]
@@ -283,39 +286,159 @@
             if 0 <= s - late < len(stages):
                 for g in stages[s - late]:
                     step(g)
+        if s < len(work):
+            work[s](i)
     own.wait()
     for g in range(groups):
         drain(g)
 
 
-def gather_rows(x, devices, chips):
+def gather_sems(chips):
     groups = 1 + 2 * (chips - 1)
     dma = pltpu.SemaphoreType.DMA
+    return [
+        dma, dma((groups,)), dma((groups,)), dma((groups, 2)), dma((groups, 2)),
+        dma((groups, 2)), dma((groups, 2)), dma((groups, 4)), dma((groups, 4)),
+    ]
+
+
+def gather_rows(x, devices, chips):
     return pl.pallas_call(
         gather_kernel,
         out_shape=jax.ShapeDtypeStruct((devices * x.shape[0], x.shape[1]), x.dtype),
         in_specs=[pl.BlockSpec(memory_space=pl.ANY)],
         out_specs=pl.BlockSpec(memory_space=pl.ANY),
-        scratch_shapes=[
-            dma, dma((groups,)), dma((groups,)), dma((groups, 2)), dma((groups, 2)),
-            dma((groups, 2)), dma((groups, 2)), dma((groups, 4)), dma((groups, 4)),
-        ],
+        scratch_shapes=gather_sems(chips),
         compiler_params=pltpu.CompilerParams(collective_id=0, has_side_effects=True),
         name="gather_rows",
     )(x)
 
 
-def pick_kernel(scale, target_ref, weight_ref, x_ref, out_ref):
+def front_kernel(
+    block, x_ref, query_ref, key_ref, value_ref, gain_ref, weight_ref,
+    out_ref, partial_ref, square_ref, own, sums, att, sum_send, sum_recv, *sems
+):
+    length, width = query_ref.shape
+    heads = width // HD
+    tall = 256 if length % 256 == 0 else length
+
+    def columns(h):
+        return pl.ds(pl.multiple_of(h * HD, HD), HD)
+
+    def span_step(h, carry):
+        feat = feature_map(key_ref[:, columns(h)])
+        own[h, :HD, :] = dot_tn(feat, value_ref[:, columns(h)]).astype(bf16)
+        keys = jnp.sum(feat.astype(f32), axis=0, keepdims=True)
+        row = lax.broadcasted_iota(jnp.int32, (16, HD), 0)
+        own[h, HD:, :] = jnp.where(row == 0, keys, 0.0).astype(bf16)
+        return carry
+
+    lax.fori_loop(0, heads, span_step, 0)
+    square_ref[...] = jnp.zeros_like(square_ref)
+    exchanged = []
+
+    def first(i, peers):
+        for j, peer in enumerate(peers):
+            copy = pltpu.make_async_remote_copy(
+                src_ref=own, dst_ref=sums.at[j], send_sem=sum_send.at[j], recv_sem=sum_recv.at[j],
+                device_id=peer, device_id_type=MESH,
+            )
+            copy.start()
+            exchanged.append(copy)
+
+    def attention(i):
+        for copy in exchanged:
+            copy.wait()
+        places = ((i // 2) * 2 + (1 - i % 2), (1 - i // 2) * 2 + i % 2, 3 - i)
+        row = lax.broadcasted_iota(jnp.int32, (block, block), 0)
+        column = lax.broadcasted_iota(jnp.int32, (block, block), 1)
+
+        def head_step(h, carry):
+            state = jnp.zeros((HD, HD), f32)
+            keys = jnp.zeros((1, HD), f32)
+            for j, place in enumerate(places):
+                earlier = place < i
+                state = state + jnp.where(earlier, sums[j, h, :HD, :].astype(f32), 0.0)
+                keys = keys + jnp.where(earlier, sums[j, h, HD:, :].astype(f32)[:1], 0.0)
+            gain = gain_ref[:, columns(h)].astype(f32)
+            for n in range(length // block):
+                at = pl.ds(n * block, block)
+                query = feature_map(query_ref[at, columns(h)])
+                key = feature_map(key_ref[at, columns(h)])
+                value = value_ref[at, columns(h)]
+                scores = jnp.where(row >= column, dot_nt(query, key), 0.0)
+                high = state.astype(bf16)
+                low = (state - high.astype(f32)).astype(bf16)
+                numerator = jnp.dot(scores.astype(bf16), value, preferred_element_type=f32)
+                numerator = numerator + jnp.dot(query, high, preferred_element_type=f32)
+                numerator = numerator + jnp.dot(query, low, preferred_element_type=f32)
+                denominator = jnp.sum(scores, axis=1, keepdims=True)
+                denominator = denominator + jnp.sum(query.astype(f32) * keys, axis=1, keepdims=True)
+                result = (numerator / denominator).astype(bf16).astype(f32)
+                att[at, columns(h)] = (result * gain).astype(bf16)
+                square_ref[at, :] = square_ref[at, :] + result * result
+                state = state + dot_tn(key, value)
+                keys = keys + jnp.sum(key.astype(f32), axis=0, keepdims=True)
+            return carry
+
+        lax.fori_loop(0, heads, head_step, 0)
+
+    def project(i):
+        def step(n, carry):
+            at = pl.ds(pl.multiple_of(n * tall, 16), tall)
+            product = jnp.dot(att[at, :], weight_ref[...], preferred_element_type=f32)
+            partial_ref[at, :] = product.astype(bf16)
+            return carry
+
+        lax.fori_loop(0, length // tall, step, 0)
+
+    gather_kernel(x_ref, out_ref, *sems, first=first, work=(attention, project))
+
+
+def front(cotangent, queries, key_heads, value_heads, gain, out_weight, devices, chips):
+    length, width = queries.shape
+    heads = width // HD
+    block = 256 if length % 256 == 0 else length
+    vmem = pl.BlockSpec(memory_space=pltpu.VMEM)
+    hbm = pl.BlockSpec(memory_space=pl.ANY)
+    dma = pltpu.SemaphoreType.DMA
+    return pl.pallas_call(
+        functools.partial(front_kernel, block),
+        out_shape=[
+            jax.ShapeDtypeStruct((devices * cotangent.shape[0], cotangent.shape[1]), bf16),
+            jax.ShapeDtypeStruct((length, out_weight.shape[1]), bf16),
+            jax.ShapeDtypeStruct((length, HD), f32),
+        ],
+        in_specs=[hbm, vmem, vmem, vmem, vmem, vmem],
+        out_specs=[hbm, vmem, vmem],
+        scratch_shapes=[
+            pltpu.VMEM((heads, HD + 16, HD), bf16),
+            pltpu.VMEM((3, heads, HD + 16, HD), bf16),
+            pltpu.VMEM((length, width), bf16),
+            dma((3,)),
+            dma((3,)),
+        ] + gather_sems(chips),
+        compiler_params=pltpu.CompilerParams(
+            collective_id=1, has_side_effects=True, vmem_limit_bytes=40 * MIB
+        ),
+        name="front",
+    )(cotangent, queries, key_heads, value_heads, gain.reshape(1, width), out_weight)
+
+
+def pick_kernel(scale, target_ref, weight_ref, x_ref, out_ref, chosen_ref):
     experts, slots = out_ref.shape[0], out_ref.shape[1]
     tokens = x_ref.shape[0]
     slot = lax.broadcasted_iota(jnp.int32, (slots, tokens), 0)
+    weights = []
     for e in range(experts):
         chosen = slot == target_ref[e : e + 1, :]
-        rows = jnp.dot(chosen.astype(f32).astype(bf16), x_ref[...], preferred_element_type=f32)
+        chosen_ref[e * slots : (e + 1) * slots, :] = chosen.astype(f32).astype(bf16)
         if scale:
-            weights = jnp.sum(jnp.where(chosen, weight_ref[e : e + 1, :], 0.0), axis=1, keepdims=True)
-            rows = rows * weights
-        out_ref[e] = rows.astype(bf16)
+            weights.append(jnp.sum(jnp.where(chosen, weight_ref[e : e + 1, :], 0.0), axis=1, keepdims=True))
+    rows = jnp.dot(chosen_ref[...], x_ref[...], preferred_element_type=f32)
+    for e in range(experts):
+        part = rows[e * slots : (e + 1) * slots]
+        out_ref[e] = (part * weights[e] if scale else part).astype(bf16)
 
 
 def pick(target, weight, x, capacity, block_rows, scale):
@@ -330,6 +453,7 @@
         out_shape=jax.ShapeDtypeStruct((experts, steps * slots, x.shape[1]), bf16),
         in_specs=[meta, meta, pl.BlockSpec((span, x.shape[1]), lambda s: (s, 0))],
         out_specs=pl.BlockSpec((experts, slots, x.shape[1]), lambda s: (0, s, 0)),
+        scratch_shapes=[pltpu.VMEM((experts * slots, span), bf16)],
         compiler_params=pltpu.CompilerParams(vmem_limit_bytes=56 * MIB),
         cost_estimate=pl.CostEstimate(
             flops=2 * experts * slots * tokens * x.shape[1],
@@ -428,15 +552,17 @@
     )
 
     if whole:
-        with jax.named_scope("gather_cotangent"):
-            cot_all = lax.all_gather(cotangent, both, axis=0, tiled=True)
-            meta = jnp.concatenate([routes.astype(f32), route_weights], axis=1).T
-            meta = lax.all_gather(meta, both, axis=0)
-
-    sums = lax.all_gather(span_sums(key_heads, value_heads), "ctx")
-    place = lax.axis_index("ctx").astype(jnp.int32).reshape(1)
-    scaled_att, squares = attend(place, queries, key_heads, value_heads, sums, out_gain)
-    partial = jnp.dot(scaled_att, out_weight, preferred_element_type=f32).astype(bf16)
+        cot_all, partial, squares = front(
+            cotangent, queries, key_heads, value_heads, out_gain, out_weight, devices, n_head // 2
+        )
+        meta = jnp.concatenate([routes.astype(f32), route_weights], axis=1).T
+        meta, partial = lax.optimization_barrier((meta, partial))
+        meta = lax.all_gather(meta, both, axis=0)
+    else:
+        sums = lax.all_gather(span_sums(key_heads, value_heads), "ctx")
+        place = lax.axis_index("ctx").astype(jnp.int32).reshape(1)
+        scaled_att, squares = attend(place, queries, key_heads, value_heads, sums, out_gain)
+        partial = jnp.dot(scaled_att, out_weight, preferred_element_type=f32).astype(bf16)
     projected = lax.psum_scatter(partial, "head", scatter_dimension=0, tiled=True).astype(f32)
     total = lax.psum_scatter(jnp.sum(squares, axis=1), "head", scatter_dimension=0, tiled=True)
     inv_rms = lax.rsqrt(total / (queries.shape[1] * n_head) + epsilon)

time: 307 us -> 315 us (1.026)
  Pallas kernels: 191 us -> 224 us
  waiting for transfers between devices: 14.9 us -> 0.02 us
  blocking collectives: 70.5 us -> 58.5 us
  local copies, waits for them, and re-layouts: 6.5 us -> 11.6 us
  matrix products: 4.5 us -> 0.14 us
    pallas_call x2 -> x1, Pallas kernels: 9.82 us -> 83.3 us  [front(): pl.pallas_call(functools.partial(front_kernel, block), out_shape=[jax.Sha...]
    pallas_call x1, Pallas kernels: 105 us -> 74.1 us  [gather_rows(): pl.pallas_call(gather_kernel, out_shape=jax.ShapeDtypeStruct((devices * x...]
    reduce_scatter x1, waiting for transfers between devices: 14.4 us -> 0.01 us  [on_device(): lax.psum_scatter(partial, 'head', scatter_dimension=0, tiled=True)]
    all_gather x1 -> x0, blocking collectives: 11.8 us -> none  [on_device(): sums = lax.all_gather(span_sums(key_heads, value_heads), 'ctx')]
    pallas_call x2, Pallas kernels: 31.2 us -> 22.5 us  [pick(): pl.pallas_call(functools.partial(pick_kernel, scale), grid=(steps,), out_...]
    unnamed x25 -> x19, local copies, waits for them, and re-layouts: 5.66 us -> 10.9 us
    dot_general x1 -> x0, matrix products: 4.36 us -> none  [on_device(): jnp.dot(scaled_att, out_weight, preferred_element_type=f32).astype(bf16)]
  transfers between devices with their start and end apart: 2 -> 1, of which waited for: 1 -> 0; matrix products, arithmetic and copies ran while one was open for 2% -> 1% of each run, Pallas kernels for 39% -> 4%
where the time goes in v2:
time: 315 us; the launch traced here: 314 us
  Pallas kernels  224 us (71%)
  blocking collectives  58.5 us (19%)
  between operations  14.8 us (5%)
  local copies, waits for them, and re-layouts  11.6 us (4%)
  other arithmetic  5.28 us (2%)
    pallas_call x1, Pallas kernels, front(): pl.pallas_call(functools.partial(front_kernel, block), out_shape=[jax.Sha...  83.3 us
    pallas_call x1, Pallas kernels, gather_rows(): pl.pallas_call(gather_kernel, out_shape=jax.ShapeDtypeStruct((devices * x...  74.1 us
    all_gather x1, blocking collectives, on_device(): meta = lax.all_gather(meta, both, axis=0)  44.5 us
    pallas_call x1, Pallas kernels, expert_grads(): pl.pallas_call(expert_kernel, grid=(experts, units // tile), out_shape=[j...  44.3 us
    pallas_call x2, Pallas kernels, pick(): pl.pallas_call(functools.partial(pick_kernel, scale), grid=(steps,), out_...  22.5 us
    unnamed x1, blocking collectives  13.9 us
    unnamed x19, local copies, waits for them, and re-layouts  10.9 us
  transfers between devices with their start and end apart: 1, of which 0 were waited for; matrix products, arithmetic and copies ran while one was open for 1% of the time, Pallas kernels for 4%

profile of v2, /device:TPU:0, one launch (start us, length us, event | category | flops | bytes accessed | tf_op | source)
XLA Modules:
  0.0 314.4 jit_solution(10447120267198535512)
XLA Ops:
  7.2 0.0 reduce-scatter.2.cloned.1.call-start
  7.2 0.7 reshape.43.gain_ref
  7.9 0.7 convert_element_type.29
  8.6 0.7 maximum_bitcast_fusion
  9.3 0.0 copy-start.1
  9.3 1.6 copy-done.1
  10.9 0.0 copy-start.2
  10.9 1.2 copy-done.2
  12.1 0.0 copy-start.3
  12.1 1.2 copy-done.3
  13.3 0.0 copy-start.4
  13.3 1.2 copy-done.4
  14.5 0.0 copy-start.5
  14.5 1.0 copy-done.5
  15.6 83.3 %front.1 = (bf16[4096,2048]{1,0:T(8,128)(2,1)}, bf16[1024,2048]{1,0:T(8,128)(2,1)S(1)}, f32[1024,128]{1,0:T(8,128)S(1)}) custom-call(bf16[128,2048]{1,0:T(8,128)(2,1)S(1)} %copy-done.5, bf16[1024,512]{1,0:T(8,128)(2,1)S(1)} %copy-done.2, bf16[1024,512]{1,0:T(8,128)(2,1)S(1)} %copy-done.3, bf16[1024,512]{1,0:T(8,128)(2,1)S(1)} %copy-done.4, ...), custom_call_target="tpu_custom_call" | custom-call | tf_op jit(solution)/shard_map/front/pallas_call | solution.py:405
  98.9 0.0 copy-start
  98.9 2.0 copy-done
  100.9 0.0 reduce-scatter.2.cloned.1.call-update
  101.0 0.0 copy-start.7
  101.0 0.7 convert_element_type.35
  101.7 44.5 %all-gather = f32[512,128]{1,0:T(8,128)S(1)} all-gather(f32[16,128]{1,0:T(8,128)S(1)} %maximum_bitcast_fusion), channel_id=2, replica_groups=mesh['ctx'=4,'head'=8] {'ctx','head'}, dimensions={0}, use_global_device_ids=true | all-gather | bytes 270336 | tf_op jit(solution)/shard_map/all_gather | solution.py:560
  146.3 0.2 fusion.6
  146.5 0.7 copy.21
  147.2 0.2 compare_reduce_fusion
  147.4 0.1 fusion.2
  147.6 0.7 copy.22
  148.2 1.2 dynamic-slice
  150.1 0.2 reduce_sum.27
  150.4 13.9 %all-reduce = f32[1024]{0:T(1024)S(1)} all-reduce(f32[1024]{0:T(1024)S(1)} %reduce_sum.27), channel_id=4, replica_groups=mesh['ctx'=4,'head'=8] {'head'}, use_global_device_ids=true, to_apply=%region_2.0.clone | all-reduce | flops 1024 | bytes 8192
  164.3 0.1 fusion.14
  164.4 11.3 %pick_scaled.1.scaled_ref = bf16[4,320,2048]{2,1,0:T(8,128)(2,1)} custom-call(s32[4,4096]{1,0:T(4,128)} %bitcast.20, f32[4,4096]{1,0:T(4,128)} %bitcast.18, bf16[4096,2048]{1,0:T(8,128)(2,1)} %get-tuple-element.16.x_ref), custom_call_target="tpu_custom_call" | custom-call | flops 5368709120 | bytes 22020096 | tf_op jit(solution)/shard_map/pick_scaled/pallas_call | solution.py:450
  175.7 0.0 reduce-scatter.2.cloned.1.call-done
  175.7 0.0 copy-done.7
  175.7 1.4 fusion.3
  177.1 0.0 copy-start.6
  177.1 1.0 fusion.5.x_ref
  178.1 74.1 %gather_rows.1.x_ref = bf16[4096,2048]{1,0:T(8,128)(2,1)} custom-call(bf16[128,2048]{1,0:T(8,128)(2,1)} %fusion.5.x_ref), custom_call_target="tpu_custom_call" | custom-call | tf_op jit(solution)/shard_map/gather_rows/pallas_call | solution.py:306
  252.2 11.1 %pick_rows.1.rows_ref = bf16[4,320,2048]{2,1,0:T(8,128)(2,1)} custom-call(s32[4,4096]{1,0:T(4,128)} %bitcast.21, f32[4,4096]{1,0:T(4,128)} %bitcast.19, bf16[4096,2048]{1,0:T(8,128)(2,1)} %gather_rows.1.x_ref), custom_call_target="tpu_custom_call" | custom-call | flops 5368709120 | bytes 22020096 | tf_op jit(solution)/shard_map/pick_rows/pallas_call | solution.py:450
  263.3 0.0 copy-done.6
  263.3 44.3 %expert_grads.1 = (bf16[4,2048,768]{2,1,0:T(8,128)(2,1)}, bf16[4,2048,768]{2,1,0:T(8,128)(2,1)}, bf16[4,768,2048]{2,1,0:T(8,128)(2,1)}) custom-call(bf16[4,320,2048]{2,1,0:T(8,128)(2,1)} %pick_rows.1.rows_ref, bf16[4,320,2048]{2,1,0:T(8,128)(2,1)} %pick_scaled.1.scaled_ref, bf16[4,2048,768]{2,1,0:T(8,128)(2,1)} %gate_ref.1, bf16[4,2048,768]{2,1,0:T(8,128)(2,1)} %up_ref.1, ...), custom_call_target="tpu_custom_call" | custom-call | flops 24159191040 | bytes 85983232 | tf_op jit(solution)/shard_map/expert_grads/pallas_call | solution.py:494
  (4 shorter events, 0.0 us)
Async XLA Ops:
  7.2 168.5 %reduce-scatter.2.cloned.1.call-start = ((), (), s32[]{:S(2)}) async-start(), calls=%async_computation.1 | async-start | bytes 4718592 | tf_op jit(solution)/shard_map/reduce_scatter | solution.py:566
  9.3 1.6 copy-start.1
  10.9 1.2 copy-start.2
  12.1 1.2 copy-start.3
  13.3 1.2 copy-start.4
  14.5 1.0 copy-start.5
  98.9 2.0 copy-start
  101.0 74.8 %copy-start.7 = (bf16[128,2048]{1,0:T(8,128)(2,1)S(1)}, bf16[128,2048]{1,0:T(8,128)(2,1)}, u32[]{:S(2)}) copy-start(bf16[128,2048]{1,0:T(8,128)(2,1)} %param.18) | copy-start | bytes 1572868
  177.1 86.2 %copy-start.6 = (bf16[128,2048]{1,0:T(8,128)(2,1)}, bf16[128,2048]{1,0:T(8,128)(2,1)S(1)}, u32[]{:S(2)}) copy-start(bf16[128,2048]{1,0:T(8,128)(2,1)S(1)} %get-tuple-element.21) | copy-start | bytes 1572868
Sparse Core Ops, SparseCore 0:
  101.1 52.5 reduce-scatter.1
